TPU v7x, 256 devices: a whole 4x4x8 slice. The times are simulated.
256 devices in a mesh: dp: 2 (over y_hi), row: 8 (over x, core), col: 16 (over y_lo, z).
Axes of the slice: x: 4, y: 4 (y_hi: 2, y_lo: 2; y = y_hi * 2 + y_lo), z: 8, core: 2. Of those that a mesh axis runs over, the one named last changes fastest.
Arguments:
- patches: bfloat16 [2, 2048, 1456], P('dp', 'col', 'row'), may hold values from -6 to 6
- queries: bfloat16 [2, 2048, 6144], P('dp', 'col', 'row'), may hold values from -6 to 6
- attn_keys: bfloat16 [2, 2048, 6144], P('dp', 'col', 'row'), may hold values from -6 to 6
- attn_values: bfloat16 [2, 2048, 6144], P('dp', 'col', 'row'), may hold values from -6 to 6
- out_weight: bfloat16 [6144, 12288], P('row', 'col'), may hold values from -0.15625 to 0.15625
- output_grad: bfloat16 [2, 2048, 12288], P('dp', 'row', 'col'), may hold values from -4 to 4
Outputs:
- query_grad: float32 [2, 2048, 6144], P('dp', 'col', 'row')
- key_grad: float32 [2, 2048, 6144], P('dp', 'col', 'row')
- value_grad: float32 [2, 2048, 6144], P('dp', 'col', 'row')
- out_weight_grad: float32 [6144, 12288], P('row', 'col')
- embed_weight_grad: float32 [1456, 12288], P('row', 'col')
All inputs are finite; a program needn't handle non-finite values.
Results may differ from a plain program's by a relative error of at most 0.025.
Values may be sent and summed in bfloat16 or wider, within the bound.
A program may use at most 128 MiB of HBM per device.

v0:
```python
import jax
import jax.numpy as jnp
from jax import lax
from jax.sharding import PartitionSpec as P

DH = 128


def contract_rows(left, right):
    return lax.dot_general(
        left, right, (((0,), (0,)), ((), ())), preferred_element_type=jnp.float32
    )


def body(patches, queries, attn_keys, attn_values, out_weight, output_grad):
    factor = DH ** (-0.5)
    local_rows = queries.shape[1]
    feature_width = queries.shape[2]
    head_count = feature_width // DH
    every_key, every_value, every_patch = (
        lax.all_gather(attn_keys, "col", axis=1, tiled=True),
        lax.all_gather(attn_values, "col", axis=1, tiled=True),
        lax.all_gather(patches, "col", axis=1, tiled=True),
    )
    local_query = queries[0].reshape(local_rows, head_count, DH)
    all_keys = every_key[0].reshape(-1, head_count, DH)
    all_values = every_value[0].reshape(-1, head_count, DH)
    scores = (
        jnp.einsum("qhd,khd->hqk", local_query, all_keys, preferred_element_type=jnp.float32)
        * factor
    )
    row_max = jnp.max(scores, axis=2, keepdims=True)
    log_total = row_max + jnp.log(jnp.sum(jnp.exp(scores - row_max), axis=2, keepdims=True))
    attn_probs = jnp.exp(scores - log_total).astype(jnp.bfloat16)
    attn_out = jnp.einsum(
        "hqk,khd->qhd", attn_probs, all_values, preferred_element_type=jnp.float32
    ).astype(jnp.bfloat16)
    out_local = attn_out.reshape(1, local_rows, feature_width)
    dense_grad = lax.all_gather(output_grad, "row", axis=1, tiled=True)[0]
    attn_grad = lax.psum_scatter(
        lax.dot_general(
            dense_grad, out_weight, (((1,), (1,)), ((), ())), preferred_element_type=jnp.float32
        ),
        "col",
        scatter_dimension=0,
        tiled=True,
    ).astype(jnp.bfloat16)
    grad_heads = attn_grad.reshape(local_rows, head_count, DH)
    prob_grad = jnp.einsum(
        "qhd,khd->hqk", grad_heads, all_values, preferred_element_type=jnp.float32
    )
    row_dot = jnp.transpose(
        jnp.sum(grad_heads.astype(jnp.float32) * attn_out.astype(jnp.float32), axis=2)
    )[:, :, None]
    score_grad = (attn_probs.astype(jnp.float32) * (prob_grad - row_dot)).astype(jnp.bfloat16)
    query_grad = (
        jnp.einsum("hqk,khd->qhd", score_grad, all_keys, preferred_element_type=jnp.float32)
        * factor
    )
    every_out = lax.all_gather(out_local, "col", axis=1, tiled=True)
    key_term = (
        jnp.einsum("hqk,qhd->khd", score_grad, local_query, preferred_element_type=jnp.float32)
        * factor
    )
    value_term = jnp.einsum(
        "hqk,qhd->khd", attn_probs, grad_heads, preferred_element_type=jnp.float32
    )
    key_sum, value_sum = (
        lax.psum_scatter(
            key_term.reshape(-1, feature_width).astype(jnp.bfloat16),
            "col",
            scatter_dimension=0,
            tiled=True,
        ).astype(jnp.float32),
        lax.psum_scatter(
            value_term.reshape(-1, feature_width).astype(jnp.bfloat16),
            "col",
            scatter_dimension=0,
            tiled=True,
        ).astype(jnp.float32),
    )
    out_part = contract_rows(every_out[0], dense_grad)
    embed_part = contract_rows(every_patch[0], dense_grad)
    out_weight_grad, embed_weight_grad = (
        lax.psum(out_part.astype(jnp.bfloat16), "dp").astype(jnp.float32),
        lax.psum(embed_part.astype(jnp.bfloat16), "dp").astype(jnp.float32),
    )
    return (
        query_grad.reshape(1, local_rows, feature_width),
        key_sum.reshape(1, local_rows, feature_width),
        value_sum.reshape(1, local_rows, feature_width),
        out_weight_grad,
        embed_weight_grad,
    )


def solution(mesh):
    placed = (
        P("dp", "col", "row"),
        P("dp", "col", "row"),
        P("dp", "col", "row"),
        P("dp", "col", "row"),
        P("row", "col"),
        P("dp", "row", "col"),
    )
    return jax.shard_map(
        body,
        mesh=mesh,
        in_specs=placed,
        out_specs=(
            P("dp", "col", "row"),
            P("dp", "col", "row"),
            P("dp", "col", "row"),
            P("row", "col"),
            P("row", "col"),
        ),
        check_vma=False,
    )
```

profile of v0, /device:TPU:6, one launch (start us, length us, event | category | flops | bytes accessed | tf_op | source)
XLA Modules:
  0.0 608.3 jit_solution(13245337660106607670)
XLA Ops:
  8.0 1.7 copy.22
  9.8 32.2 %all-gather.7.cloned.1.call-done = bf16[1,2048,768]{2,1,0:T(8,128)(2,1)} async-done(((bf16[1,256,768]{2,1,0:T(8,128)(2,1)}), bf16[1,2048,768]{2,1,0:T(8,128)(2,1)}) %all-gather.7.cloned.1.call-update) | async-done | bytes 3145744 | tf_op jit(solution)/shard_map/all_gather | solution.py:39
  42.0 7.2 %fusion.5 = f32[2048,768]{1,0:T(8,128)} fusion(bf16[768,768]{1,0:T(8,128)(2,1)S(1)} %copy-done, bf16[1,2048,768]{2,1,0:T(8,128)(2,1)} %all-gather.7.cloned.1.call-done), kind=kOutput, calls=%fused_computation.11 | convolution fusion | flops 2415919104 | bytes 10616832 | tf_op jit(solution)/shard_map/dot_general | solution.py:41
  49.2 0.8 copy-done.3
  50.1 0.8 copy.26
  51.2 73.3 %all-gather.5.cloned.1.call-done = bf16[1,2048,768]{1,2,0:T(8,128)(2,1)} async-done(((bf16[1,128,768]{1,2,0:T(8,128)(2,1)}), bf16[1,2048,768]{1,2,0:T(8,128)(2,1)}) %all-gather.5.cloned.1.call-update) | async-done | bytes 3145744 | tf_op jit(solution)/shard_map/all_gather | solution.py:21
  124.4 3.0 multiply_reduce_fusion
  127.4 1.2 exponential_reduce_fusion
  128.6 2.6 exponential_convert_fusion
  131.2 83.0 %reduce-scatter.4.cloned.1.call-done = f32[128,768]{1,0:T(8,128)} async-done(((f32[2048,768]{1,0:T(8,128)}), f32[128,768]{1,0:T(8,128)}) %reduce-scatter.4.cloned.1.call-update) | async-done | bytes 393232 | tf_op jit(solution)/shard_map/reduce_scatter | solution.py:40
  214.2 1.0 convert_element_type.58
  215.4 76.4 %all-gather.9.cloned.1.call-done = bf16[1,2048,768]{1,2,0:T(8,128)(2,1)} async-done(((bf16[1,128,768]{1,2,0:T(8,128)(2,1)}), bf16[1,2048,768]{1,2,0:T(8,128)(2,1)}) %all-gather.9.cloned.1.call-update) | async-done | bytes 3145744 | tf_op jit(solution)/shard_map/all_gather | solution.py:22
  291.8 4.5 multiply_reduce_fusion.1
  296.3 3.9 multiply_convert_fusion.1
  300.3 2.7 multiply_convert_fusion
  302.9 4.7 copy.29
  307.7 4.6 convolution_convert_fusion
  312.2 4.7 copy.30
  317.0 0.7 copy-done.5
  317.7 39.6 %all_gather.19 = bf16[1,2048,182]{1,2,0:T(8,128)(2,1)S(1)} all-gather(bf16[1,128,182]{1,2,0:T(8,128)(2,1)S(1)} %copy-done.5), channel_id=1, replica_groups=mesh['dp'=2,'row'=8,'col'=16] {'col'}, dimensions={1}, use_global_device_ids=true | all-gather | bytes 792064 | tf_op jit(solution)/shard_map/all_gather | solution.py:23
  357.3 3.4 fusion.12
  360.7 19.5 %all-gather.11.cloned.1.call-done = bf16[1,2048,768]{1,2,0:T(8,128)(2,1)} async-done(((bf16[1,128,768]{1,2,0:T(8,128)(2,1)}), bf16[1,2048,768]{1,2,0:T(8,128)(2,1)}) %all-gather.11.cloned.1.call-update) | async-done | bytes 3145744 | tf_op jit(solution)/shard_map/all_gather | solution.py:60
  380.2 6.5 %fusion.7 = bf16[768,768]{1,0:T(8,128)(2,1)} fusion(bf16[1,2048,768]{2,1,0:T(8,128)(2,1)} %all-gather.7.cloned.1.call-done, bf16[1,2048,768]{1,2,0:T(8,128)(2,1)} %all-gather.11.cloned.1.call-done), kind=kOutput, calls=%fused_computation.13 | convolution fusion | flops 2416508928 | bytes 7471104 | tf_op jit(solution)/shard_map/dot_general | solution.py:10
  386.7 3.8 convolution_multiply_fusion
  390.5 0.9 copy.31
  391.4 68.6 %reduce-scatter.6.cloned.1.call-done = bf16[128,768]{1,0:T(8,128)(2,1)} async-done(((bf16[2048,768]{1,0:T(8,128)(2,1)}), bf16[128,768]{1,0:T(8,128)(2,1)}) %reduce-scatter.6.cloned.1.call-update) | async-done | bytes 196624 | tf_op jit(solution)/shard_map/reduce_scatter | solution.py:69
  460.0 1.7 bitcast_convert_fusion.1
  461.7 74.5 %reduce-scatter.8.cloned.1.call-done = bf16[128,768]{1,0:T(8,128)(2,1)} async-done(((bf16[2048,768]{1,0:T(8,128)(2,1)}), bf16[128,768]{1,0:T(8,128)(2,1)}) %reduce-scatter.8.cloned.1.call-update) | async-done | bytes 196624 | tf_op jit(solution)/shard_map/reduce_scatter | solution.py:75
  536.2 1.7 bitcast_convert_fusion
  537.9 59.9 %all-reduce.3.cloned.1.call-done = (bf16[768,768]{1,0:T(8,128)(2,1)}, bf16[182,768]{1,0:T(8,128)(2,1)}) async-done(((bf16[768,768]{1,0:T(8,128)(2,1)}, bf16[182,768]{1,0:T(8,128)(2,1)}), (bf16[768,768]{1,0:T(8,128)(2,1)}, bf16[182,768]{1,0:T(8,128)(2,1)})) %all-reduce.3.cloned.1.call-update) | async-done | bytes 1459216 | tf_op jit(solution)/shard_map/psum | solution.py:85
  597.8 2.9 convert_element_type.71
  600.6 0.8 convert_element_type.73
  (29 shorter events, 1.5 us)
Async XLA Ops:
  7.2 34.8 %copy-start = (bf16[768,768]{1,0:T(8,128)(2,1)S(1)}, bf16[768,768]{1,0:T(8,128)(2,1)}, u32[]{:S(2)}) copy-start(bf16[768,768]{1,0:T(8,128)(2,1)} %param.10) | copy-start | bytes 3538948
  7.2 34.8 %all-gather.7.cloned.1.call-start = ((), (), s32[]{:S(2)}) async-start(), calls=%async_computation.4 | async-start | bytes 3538944 | tf_op jit(solution)/shard_map/all_gather | solution.py:39
  7.9 116.5 %all-gather.5.cloned.1.call-start = ((), (), s32[]{:S(2)}) async-start(), calls=%async_computation.3 | async-start | bytes 3342336 | tf_op jit(solution)/shard_map/all_gather | solution.py:21
  9.7 204.5 %reduce-scatter.4.cloned.1.call-start = ((), (), s32[]{:S(2)}) async-start(), calls=%async_computation.5 | async-start | bytes 6684672 | tf_op jit(solution)/shard_map/reduce_scatter | solution.py:40
  49.2 0.9 copy-start.3
  49.2 1.8 copy-start.4
  49.2 242.6 %all-gather.9.cloned.1.call-start = ((), (), s32[]{:S(2)}) async-start(), calls=%async_computation.6 | async-start | bytes 3342336 | tf_op jit(solution)/shard_map/all_gather | solution.py:22
  50.9 329.3 %all-gather.11.cloned.1.call-start = ((), (), s32[]{:S(2)}) async-start(), calls=%async_computation.9 | async-start | bytes 3342336 | tf_op jit(solution)/shard_map/all_gather | solution.py:60
  296.3 163.7 %reduce-scatter.6.cloned.1.call-start = ((), (), s32[]{:S(2)}) async-start(), calls=%async_computation.7 | async-start | bytes 3342336 | tf_op jit(solution)/shard_map/reduce_scatter | solution.py:69
  300.3 2.7 copy-start.1
  307.6 228.5 %reduce-scatter.8.cloned.1.call-start = ((), (), s32[]{:S(2)}) async-start(), calls=%async_computation.8 | async-start | bytes 3342336 | tf_op jit(solution)/shard_map/reduce_scatter | solution.py:75
  316.9 0.8 copy-start.5
  316.9 280.8 %all-reduce.3.cloned.1.call-start = ((), (), s32[]{:S(2)}) async-start(), calls=%async_computation.10 | async-start | bytes 2924544 | tf_op jit(solution)/shard_map/psum | solution.py:85
  597.8 2.9 copy-start.2
Sparse Core Ops, SparseCore 0:
  9.8 32.0 all-gather.6
  44.3 80.1 all-gather.4
  127.0 87.1 reduce-scatter.3
  216.3 75.3 all-gather.8
  296.4 83.7 all-gather.10
  382.6 77.3 reduce-scatter.5
  462.5 73.5 reduce-scatter.7
  539.4 58.3 all-reduce.2
where the time goes:
time: 610 us; the launch traced here: 608 us
  waiting for transfers between devices  488 us (80%)
  blocking collectives  39.6 us (6%)
  matrix products  39.5 us (6%)
  local copies, waits for them, and re-layouts  14.7 us (2%)
  between operations  14.2 us (2%)
  other arithmetic  11.9 us (2%)
    reduce_scatter x1, waiting for transfers between devices, body(): lax.psum_scatter(lax.dot_general(dense_grad, out_weight, (((1,), (1,)), (...  83 us
    all_gather x1, waiting for transfers between devices, body(): lax.all_gather(attn_values, 'col', axis=1, tiled=True)  76.4 us
    reduce_scatter x1, waiting for transfers between devices, body(): lax.psum_scatter(value_term.reshape(-1, feature_width).astype(jnp.bfloat1...  74.5 us
    all_gather x1, waiting for transfers between devices, body(): lax.all_gather(attn_keys, 'col', axis=1, tiled=True)  73.3 us
    reduce_scatter x1, waiting for transfers between devices, body(): lax.psum_scatter(key_term.reshape(-1, feature_width).astype(jnp.bfloat16)...  68.6 us
    psum x1, waiting for transfers between devices, body(): lax.psum(out_part.astype(jnp.bfloat16), 'dp').astype(jnp.float32)  59.9 us
    all_gather x1, blocking collectives, body(): lax.all_gather(patches, 'col', axis=1, tiled=True)  39.6 us
    all_gather x1, waiting for transfers between devices, body(): dense_grad = lax.all_gather(output_grad, 'row', axis=1, tiled=True)[0]  32.2 us
  transfers between devices with their start and end apart: 8, of which 8 were waited for; matrix products, arithmetic and copies ran while one was open for 9% of the time, Pallas kernels for 0%

commit v1 on v0

v1 whole, which is shorter than its diff:
```python
import math

import jax
import jax.numpy as jnp
from jax import lax
from jax.experimental import pallas as pl
from jax.experimental.pallas import tpu as pltpu
from jax.sharding import PartitionSpec as P

DH = 128
MESH = pl.DeviceIdType.MESH
F32 = jnp.float32
BF16 = jnp.bfloat16
FACTOR = DH ** (-0.5)
OWNER_Y = (0, 1, 0, 0, 1, 0)
OWNER_Z = (0, 0, 2, 4, 4, 6)
RS_GAP = 2
AG_GAP = 2
FWD_AT = 6


def plain_dot(left, right):
    return lax.dot_general(left, right, (((1,), (0,)), ((), ())), preferred_element_type=F32)


def dot_t(left, right):
    return lax.dot_general(left, right, (((1,), (1,)), ((), ())), preferred_element_type=F32)


def kernel(
    q_ref, k_ref, v_ref, p_ref, w_ref, g_ref,
    qg_ref, kg_ref, vg_ref, ow_ref, ew_ref,
    gall, wt, qkv, k_t, v_t, rs_in, rs_y, rs_out, d_out, ao, e_buf, s_buf, inv_buf,
    kacc, vacc, og, og_in, ow_out, ow_in, pat, ew_out, ew_in,
    in_s, in_r, g_s, g_r, p_s, p_r, rs_s, rs_r, rsy_r, ag_s, ag_r, ow_s, ow_r, ew_s, ew_r, og_s, og_r,
):
    dp, row, col = lax.axis_index("dp"), lax.axis_index("row"), lax.axis_index("col")
    x, p = lax.div(row, 2), lax.rem(row, 2)
    y, z = lax.div(col, 8), lax.rem(col, 8)

    def mirror(zz):
        return zz * (1 - p) + p * lax.rem(9 - zz, 8)

    zp = mirror(z)
    step_x = 1 - 2 * p

    def at(yy, zz):
        return (dp, row, yy * 8 + mirror(zz))

    def at_x(offset):
        return (dp, lax.rem(x + offset + 4, 4) * 2 + p, col)

    z_up, z_down = lax.rem(zp + 1, 8), lax.rem(zp + 7, 8)
    sibling = (dp, row + 1 - 2 * p, col)
    other_dp = (1 - dp, row, col)
    middle_z = lax.div(lax.rem(zp, 4), 2)
    own_head = 3 * lax.div(zp, 4) + 2 * middle_z + y * (1 - middle_z)
    is_owner = jnp.logical_and(lax.rem(zp, 2) == 0, jnp.logical_or(y == 0, lax.rem(zp, 4) == 0))

    def remote(src, dst, send, recv, device):
        return pltpu.make_async_remote_copy(
            src_ref=src, dst_ref=dst, send_sem=send, recv_sem=recv, device_id=device, device_id_type=MESH
        )

    barrier = pltpu.get_barrier_semaphore()
    for k in range(1, 16):
        pl.semaphore_signal(barrier, inc=1, device_id=(dp, row, lax.rem(col + k, 16)), device_id_type=MESH)
    for device in (at_x(1), at_x(-1), sibling, other_dp):
        pl.semaphore_signal(barrier, inc=1, device_id=device, device_id_type=MESH)
    gall[x, p] = g_ref[...]
    pat[col] = p_ref[...]
    for h in range(6):
        wt[h] = w_ref[h].T
    pl.semaphore_wait(barrier, 19)

    sources = (q_ref, k_ref, v_ref)

    def in_copy(t, h):
        return remote(
            sources[t].at[:, h * DH : (h + 1) * DH], qkv.at[t, col], in_s.at[t, h], in_r.at[t],
            at(OWNER_Y[h], OWNER_Z[h]),
        )

    def owns(h):
        return jnp.logical_and(y == OWNER_Y[h], zp == OWNER_Z[h])

    def g_copy(n, xx, pp, device):
        block = lax.rem(xx + 8, 4)
        return remote(gall.at[block, pp], gall.at[block, pp], g_s.at[n], g_r.at[block, pp], device)

    def g_wait(xx, pp):
        block = lax.rem(xx + 8, 4)
        pltpu.make_async_copy(gall.at[block, pp], gall.at[block, pp], g_r.at[block, pp]).wait()

    g_sends = (
        (0, x, sibling),
        (1, x, at_x(step_x)),
        (2, x, at_x(-step_x)),
        (3, x - step_x, at_x(step_x)),
        (4, x - step_x, sibling),
        (5, x + step_x, sibling),
        (6, x + 2, sibling),
    )

    def g_start(n):
        g_copy(n, g_sends[n][1], p, g_sends[n][2]).start()

    for n in range(3):
        g_start(n)

    for h in range(6):
        @pl.when(owns(h))
        def _():
            for t in range(3):
                pltpu.make_async_copy(
                    sources[t].at[:, h * DH : (h + 1) * DH], qkv.at[t, col], in_r.at[t]
                ).start()

        @pl.when(jnp.logical_not(owns(h)))
        def _():
            for t in range(3):
                in_copy(t, h).start()

    def p_copy(kind, block, device):
        return remote(pat.at[block], pat.at[block], p_s.at[kind, block], p_r.at[block], device)

    def p_wait(block):
        pltpu.make_async_copy(pat.at[block], pat.at[block], p_r.at[block]).wait()

    def block_at(offset):
        return y * 8 + mirror(lax.rem(zp + offset + 8, 8))

    p_copy(0, col, at(y, z_up)).start()
    p_copy(1, col, at(y, z_down)).start()
    p_copy(2, col, at(1 - y, zp)).start()

    def patch_step(k):
        up_block = block_at(-k)
        p_wait(up_block)

        @pl.when(k < 4)
        def _():
            p_copy(0, up_block, at(y, z_up)).start()

        p_copy(2, up_block, at(1 - y, zp)).start()

        @pl.when(k < 4)
        def _():
            down_block = block_at(k)
            p_wait(down_block)

            @pl.when(k < 3)
            def _():
                p_copy(1, down_block, at(y, z_down)).start()

            p_copy(2, down_block, at(1 - y, zp)).start()

    def heads_of(t, j):
        exists = jnp.logical_and(lax.rem(t, 2) == 0, jnp.logical_or(j == 0, lax.rem(t, 4) == 0))
        middle = lax.div(lax.rem(t, 4), 2)
        h = 3 * lax.div(t, 4) + 2 * middle + j * (1 - middle)
        return exists, jnp.minimum(h, 5)

    def owner_y(h):
        return lax.div(lax.rem(h, 3) + 1, 2) * (1 - lax.div(lax.rem(h, 3), 2))

    def partial(h, c):
        return plain_dot(gall[c].reshape(512, 768), wt[h])

    def rs_wait(kind, h, c):
        pltpu.make_async_copy(rs_in.at[kind, h, c], rs_in.at[kind, h, c], rs_r.at[kind, h, c]).wait()

    def rs_chain(i, q):
        c = chunk_of(i)
        dist = 4 - lax.div(q + 1, 2)
        is_min = (1 - lax.rem(q, 2)) * jnp.minimum(q, 1)
        t = lax.rem(zp + is_min * (8 - dist) + (1 - is_min) * dist, 8)
        up = dist + is_min < 4
        nxt = at(y, lax.rem(zp + 1 + 6 * is_min, 8))
        for j in range(2):
            exists, h = heads_of(t, j)

            @pl.when(exists)
            def _():
                total = partial(h, c)

                @pl.when(up)
                def _():
                    rs_wait(is_min, h, c)
                    rs_out[h, c] = (total + rs_in[is_min, h, c].astype(F32)).astype(BF16)

                @pl.when(jnp.logical_not(up))
                def _():
                    rs_out[h, c] = total.astype(BF16)

                remote(
                    rs_out.at[h, c], rs_in.at[is_min, h, c], rs_s.at[h, c], rs_r.at[is_min, h, c], nxt
                ).start()

    def rs_root(i):
        c = chunk_of(i)
        for j in range(2):
            exists, h = heads_of(zp, j)

            @pl.when(jnp.logical_and(exists, owner_y(h) != y))
            def _():
                total = partial(h, c)
                rs_wait(0, h, c)
                rs_wait(1, h, c)
                total = total + rs_in[0, h, c].astype(F32) + rs_in[1, h, c].astype(F32)
                rs_out[h, c] = total.astype(BF16)
                remote(rs_out.at[h, c], rs_y.at[c], rs_s.at[h, c], rsy_r.at[c], at(1 - y, zp)).start()

        @pl.when(is_owner)
        def _():
            total = partial(own_head, c)
            rs_wait(0, own_head, c)
            rs_wait(1, own_head, c)
            total = total + rs_in[0, own_head, c].astype(F32) + rs_in[1, own_head, c].astype(F32)
            pltpu.make_async_copy(rs_y.at[c], rs_y.at[c], rsy_r.at[c]).wait()
            total = total + rs_y[c].astype(F32)
            d_out[c] = total.astype(BF16)

    def chunk_of(i):
        return lax.rem(x + i + lax.div(i, 2) * (1 - 2 * lax.div(i, 3)), 4)

    def fwd_setup():
        for t in range(3):
            pltpu.make_async_copy(qkv.at[t], qkv.at[t], in_r.at[t]).wait()
        for b in range(4):
            k_t[b] = qkv[1, 4 * b : 4 * b + 4].reshape(512, DH).T
            v_t[b] = qkv[2, 4 * b : 4 * b + 4].reshape(512, DH).T

    def queries_of(n):
        return qkv[0, pl.ds(2 * n, 2)].reshape(256, DH)

    def fwd_block(n):
        query = queries_of(n)
        top = None
        for b in range(4):
            s = dot_t(qkv[1, 4 * b : 4 * b + 4].reshape(512, DH), query)
            s_buf[b] = s
            high = jnp.max(s, axis=0, keepdims=True)
            top = high if top is None else jnp.maximum(top, high)
        total, out = None, None
        for b in range(4):
            e = jnp.exp2((s_buf[b] - top) * (FACTOR * math.log2(math.e)))
            part = jnp.sum(e, axis=0, keepdims=True)
            total = part if total is None else total + part
            e = e.astype(BF16)
            e_buf[n, b] = e
            o = plain_dot(v_t[b], e)
            out = o if out is None else out + o
        inv = 1.0 / total
        inv_buf[n] = inv
        ao[own_head, lax.div(n, 2), lax.rem(n, 2)] = (out * inv).astype(BF16)

    def bwd_block(n):
        query = queries_of(n)
        c, half = lax.div(n, 2), lax.rem(n, 2)
        d = d_out[c, pl.ds(pl.multiple_of(half * 256, 256), 256)].astype(F32).T
        d = (d * inv_buf[n]).astype(BF16)
        dot_row = jnp.sum(d.astype(F32) * ao[own_head, c, half].astype(F32), axis=0, keepdims=True)
        grad = None
        for b in range(4):
            rows = slice(4 * b, 4 * b + 4)
            e = e_buf[n, b]
            dprob = plain_dot(qkv[2, rows].reshape(512, DH), d)
            ds = ((dprob - dot_row) * e.astype(F32)).astype(BF16)
            vacc[b] += dot_t(e, d)
            kacc[b] += plain_dot(ds, query)
            part = plain_dot(k_t[b], ds)
            grad = part if grad is None else grad + part
        og[0, pl.ds(2 * n, 2)] = (grad * FACTOR).T.astype(BF16).reshape(2, 128, DH)

    g_wait(x, 1 - p)

    @pl.loop(0, 3 * RS_GAP + 8)
    def _(tau):
        @pl.when(tau == RS_GAP)
        def _():
            g_wait(x - step_x, p)
            g_start(3)
            g_start(4)
            g_wait(x + step_x, p)
            g_start(5)
            g_wait(x - step_x, 1 - p)
            g_wait(x + step_x, 1 - p)

        @pl.when(tau == 3 * RS_GAP)
        def _():
            g_wait(x + 2, p)
            g_start(6)
            g_wait(x + 2, 1 - p)

        @pl.when(jnp.logical_and(tau >= RS_GAP, tau < RS_GAP + 4))
        def _():
            patch_step(tau - RS_GAP + 1)

        @pl.loop(0, 4)
        def _(i):
            q = tau - RS_GAP * i

            @pl.when(jnp.logical_and(q >= 0, q < 7))
            def _():
                rs_chain(i, q)

            @pl.when(q == 7)
            def _():
                rs_root(i)

        @pl.when(jnp.logical_and(is_owner, tau >= FWD_AT))
        def _():
            @pl.when(tau == FWD_AT)
            def _():
                fwd_setup()

            fwd_block(tau - FWD_AT)

    @pl.loop(0, 8)
    def _(k):
        p_wait((1 - y) * 8 + k)

    def ew_add(k, total):
        c, n = lax.div(k, 4), lax.rem(k, 4)
        tokens = gall[c, lax.div(n, 2), pl.ds(pl.multiple_of(lax.rem(n, 2) * 128, 128), 128)]
        return total + plain_dot(pat[k], tokens)

    ew_out[...] = lax.fori_loop(0, 16, ew_add, jnp.zeros((192, 768), F32)).astype(BF16)
    ew_copy = remote(ew_out, ew_in, ew_s, ew_r, other_dp)
    ew_copy.start()

    def ag_copy(kind, h, c, device):
        return remote(ao.at[h, c], ao.at[h, c], ag_s.at[kind, h, c], ag_r.at[h, c], device)

    def ag_wait(h, c):
        pltpu.make_async_copy(ao.at[h, c], ao.at[h, c], ag_r.at[h, c]).wait()

    def ow_copy(h):
        return remote(ow_out.at[h], ow_in.at[h], ow_s.at[h], ow_r.at[h], other_dp)

    def finish_head(h):
        total = None
        for c in range(4):
            for half in range(2):
                part = plain_dot(ao[h, c, half], gall[c, half])
                total = part if total is None else total + part
        ow_out[h] = total.astype(BF16)
        ow_copy(h).start()

    def ag_item(c, q):
        dist = lax.div(q + 1, 2)
        is_min = (1 - lax.rem(q, 2)) * jnp.minimum(q, 1)
        t = lax.rem(zp + is_min * dist + (1 - is_min) * (8 - dist), 8)
        here = q == 0
        for j in range(2):
            exists, h = heads_of(t, j)

            @pl.when(exists)
            def _():
                root = jnp.logical_and(here, owner_y(h) == y)

                @pl.when(jnp.logical_not(root))
                def _():
                    ag_wait(h, c)

                @pl.when(root)
                def _():
                    ag_copy(2, h, c, at(1 - y, zp)).start()

                @pl.when(jnp.logical_and(is_min == 0, dist < 4))
                def _():
                    ag_copy(0, h, c, at(y, z_up)).start()

                @pl.when(jnp.logical_or(here, jnp.logical_and(is_min == 1, dist < 3)))
                def _():
                    ag_copy(1, h, c, at(y, z_down)).start()

                @pl.when(c == 3)
                def _():
                    finish_head(h)

    @pl.when(is_owner)
    def _():
        kacc[...] = jnp.zeros_like(kacc)
        vacc[...] = jnp.zeros_like(vacc)

    @pl.loop(0, 3 * AG_GAP + 8)
    def _(tau):
        @pl.loop(0, 4)
        def _(c):
            q = tau - AG_GAP * c

            @pl.when(jnp.logical_and(q >= 0, q < 8))
            def _():
                ag_item(c, q)

        @pl.when(jnp.logical_and(is_owner, tau < 8))
        def _():
            bwd_block(tau)

    def og_copy(t, k):
        return remote(og.at[t, k], og_in.at[t, own_head], og_s.at[t, k], og_r.at[t], (dp, row, k))

    @pl.when(is_owner)
    def _():
        for b in range(4):
            og[1, 4 * b : 4 * b + 4] = (kacc[b] * FACTOR).astype(BF16).reshape(4, 128, DH)
            og[2, 4 * b : 4 * b + 4] = vacc[b].astype(BF16).reshape(4, 128, DH)

        for t in range(3):
            pltpu.make_async_copy(og.at[t, col], og_in.at[t, own_head], og_r.at[t]).start()

        @pl.loop(1, 16)
        def _(k):
            for t in range(3):
                og_copy(t, lax.rem(col + k, 16)).start()

    ew_copy.wait()
    ew_ref[...] = ew_out[...].astype(F32) + ew_in[...].astype(F32)

    @pl.loop(0, 6)
    def _(h):
        ow_copy(h).wait()
        ow_ref[h] = ow_out[h].astype(F32) + ow_in[h].astype(F32)

    for t, ref in enumerate((qg_ref, kg_ref, vg_ref)):
        pltpu.make_async_copy(og_in.at[t], og_in.at[t], og_r.at[t]).wait()
        for h in range(6):
            ref[:, h * DH : (h + 1) * DH] = og_in[t, h].astype(F32)

    for h in range(6):
        @pl.when(jnp.logical_not(owns(h)))
        def _():
            for t in range(3):
                in_copy(t, h).wait_send()
    for n in range(7):
        g_copy(n, g_sends[n][1], p, g_sends[n][2]).wait_send()

    @pl.loop(0, 8)
    def _(k):
        block = block_at(k)
        p_copy(2, block, at(1 - y, zp)).wait_send()

        @pl.when(jnp.logical_or(k == 0, k > 4))
        def _():
            p_copy(0, block, at(y, z_up)).wait_send()

        @pl.when(k < 3)
        def _():
            p_copy(1, block, at(y, z_down)).wait_send()

    @pl.loop(0, 6)
    def _(h):
        zh = 4 * lax.div(h, 3) + 2 * lax.div(lax.rem(h, 3), 2)
        rel = lax.rem(zp - zh + 8, 8)
        root = jnp.logical_and(rel == 0, owner_y(h) == y)

        @pl.loop(0, 4)
        def _(c):
            @pl.when(jnp.logical_not(root))
            def _():
                pltpu.make_async_copy(rs_out.at[h, c], rs_out.at[h, c], rs_s.at[h, c]).wait()

            @pl.when(root)
            def _():
                ag_copy(2, h, c, at(1 - y, zp)).wait_send()

            @pl.when(rel < 4)
            def _():
                ag_copy(0, h, c, at(y, z_up)).wait_send()

            @pl.when(jnp.logical_or(rel == 0, rel > 5))
            def _():
                ag_copy(1, h, c, at(y, z_down)).wait_send()

    @pl.when(is_owner)
    def _():
        @pl.loop(1, 16)
        def _(k):
            for t in range(3):
                og_copy(t, lax.rem(col + k, 16)).wait_send()


def body(patches, queries, attn_keys, attn_values, out_weight, output_grad):
    patch_t = jnp.pad(patches[0].T, ((0, 10), (0, 0)))
    dma = pltpu.SemaphoreType.DMA
    scratch = [
        pltpu.VMEM((4, 2, 256, 768), BF16),
        pltpu.VMEM((6, 768, DH), BF16),
        pltpu.VMEM((3, 16, 128, DH), BF16),
        pltpu.VMEM((4, DH, 512), BF16),
        pltpu.VMEM((4, DH, 512), BF16),
        pltpu.VMEM((2, 6, 4, 512, DH), BF16),
        pltpu.VMEM((4, 512, DH), BF16),
        pltpu.VMEM((6, 4, 512, DH), BF16),
        pltpu.VMEM((4, 512, DH), BF16),
        pltpu.VMEM((6, 4, 2, DH, 256), BF16),
        pltpu.VMEM((8, 4, 512, 256), BF16),
        pltpu.VMEM((4, 512, 256), F32),
        pltpu.VMEM((8, 1, 256), F32),
        pltpu.VMEM((4, 512, DH), F32),
        pltpu.VMEM((4, 512, DH), F32),
        pltpu.VMEM((3, 16, 128, DH), BF16),
        pltpu.VMEM((3, 6, 128, DH), BF16),
        pltpu.VMEM((6, 128, 768), BF16),
        pltpu.VMEM((6, 128, 768), BF16),
        pltpu.VMEM((16, 192, 128), BF16),
        pltpu.VMEM((192, 768), BF16),
        pltpu.VMEM((192, 768), BF16),
        dma((3, 6)), dma((3,)),
        dma((7,)), dma((4, 2)),
        dma((3, 16)), dma((16,)),
        dma((6, 4)), dma((2, 6, 4)), dma((4,)),
        dma((3, 6, 4)), dma((6, 4)),
        dma((6,)), dma((6,)),
        dma, dma,
        dma((3, 16)), dma((3,)),
    ]
    vmem = pl.BlockSpec(memory_space=pltpu.VMEM)
    qg, kg, vg, ow, ew = pl.pallas_call(
        kernel,
        out_shape=[jax.ShapeDtypeStruct((128, 768), F32)] * 3
        + [jax.ShapeDtypeStruct((6, 128, 768), F32), jax.ShapeDtypeStruct((192, 768), F32)],
        in_specs=[vmem] * 6,
        out_specs=[vmem] * 5,
        scratch_shapes=scratch,
        compiler_params=pltpu.CompilerParams(
            collective_id=0, has_side_effects=True, vmem_limit_bytes=60 * 2**20
        ),
        cost_estimate=pl.CostEstimate(flops=8 * 10**9, bytes_accessed=8 * 10**6, transcendentals=4 * 10**6),
    )(
        queries[0], attn_keys[0], attn_values[0], patch_t,
        out_weight.reshape(6, DH, 768), output_grad[0],
    )
    return (qg[None], kg[None], vg[None], ow.reshape(768, 768), ew[:182])


def solution(mesh):
    placed = (
        P("dp", "col", "row"),
        P("dp", "col", "row"),
        P("dp", "col", "row"),
        P("dp", "col", "row"),
        P("row", "col"),
        P("dp", "row", "col"),
    )
    return jax.shard_map(
        body,
        mesh=mesh,
        in_specs=placed,
        out_specs=(
            P("dp", "col", "row"),
            P("dp", "col", "row"),
            P("dp", "col", "row"),
            P("row", "col"),
            P("row", "col"),
        ),
        check_vma=False,
    )
```

time: 610 us -> 192 us (0.31)
  the two profiles are of different devices: /device:TPU:6 before, /device:TPU:20 now
where the time goes in v1:
time: 192 us
  Pallas kernels  181 us (94%)
  local copies, waits for them, and re-layouts  10.2 us (5%)
    pallas_call x1, Pallas kernels, body(): pl.pallas_call(kernel, out_shape=[jax.ShapeDtypeStruct((128, 768), F32)]...  181 us
    unnamed x6, local copies, waits for them, and re-layouts  6.71 us

profile of v1, /device:TPU:20, one launch (start us, length us, event | category | flops | bytes accessed | tf_op | source)
XLA Modules:
  0.0 191.5 jit_solution(4746810816424422373)
XLA Ops:
  0.6 1.4 pad.4.p_ref
  2.1 180.7 %shard_map.101 = (f32[128,768]{1,0:T(8,128)}, f32[128,768]{1,0:T(8,128)}, f32[128,768]{1,0:T(8,128)}, f32[6,128,768]{2,1,0:T(8,128)}, f32[192,768]{1,0:T(8,128)}) custom-call(bf16[128,768]{1,0:T(8,128)(2,1)} %bitcast.19, bf16[128,768]{1,0:T(8,128)(2,1)} %bitcast.20, bf16[128,768]{1,0:T(8,128)(2,1)} %bitcast.21, bf16[192,128]{1,0:T(8,128)(2,1)} %pad.4.p_ref, ...), custom_call_target="tpu_custom_call" | custom-call | flops 8000000000 | bytes 8000000 | tf_op jit(solution)/shard_map/pallas_call | solution.py:521
  182.8 0.0 copy-start
  182.8 2.0 %slice.3 = f32[182,768]{1,0:T(8,128)} slice(f32[192,768]{1,0:T(8,128)} %get-tuple-element.14), slice={[0:182], [0:768]} | slice | bytes 1118208 | tf_op jit(solution)/shard_map/slice | solution.py:536
  184.8 1.8 copy.15
  186.6 1.8 copy.16
  188.4 1.8 copy.17
  190.1 0.0 copy-done
  190.1 1.4 copy.18
Async XLA Ops:
  182.8 7.4 %copy-start = (f32[6,128,768]{2,1,0:T(8,128)S(1)}, f32[6,128,768]{2,1,0:T(8,128)}, u32[]{:S(2)}) copy-start(f32[6,128,768]{2,1,0:T(8,128)} %get-tuple-element.13) | copy-start | bytes 7077892

commit v2 on v1

--- a/solution.py
+++ b/solution.py
@@ -14,9 +14,11 @@
 FACTOR = DH ** (-0.5)
 OWNER_Y = (0, 1, 0, 0, 1, 0)
 OWNER_Z = (0, 0, 2, 4, 4, 6)
-RS_GAP = 2
-AG_GAP = 2
-FWD_AT = 6
+FWD_AT = 1
+AG_AT = 2
+BWD_AT = 7
+SEND_AT = 11
+STEPS = 13
 
 
 def plain_dot(left, right):
@@ -29,9 +31,9 @@
 
 def kernel(
     q_ref, k_ref, v_ref, p_ref, w_ref, g_ref,
-    qg_ref, kg_ref, vg_ref, ow_ref, ew_ref,
+    qkv_ref, ow_ref, ew_ref,
     gall, wt, qkv, k_t, v_t, rs_in, rs_y, rs_out, d_out, ao, e_buf, s_buf, inv_buf,
-    kacc, vacc, og, og_in, ow_out, ow_in, pat, ew_out, ew_in,
+    kacc, vacc, ow_acc, og, og_in, ow_out, ow_in, pat, ew_out, ew_in,
     in_s, in_r, g_s, g_r, p_s, p_r, rs_s, rs_r, rsy_r, ag_s, ag_r, ow_s, ow_r, ew_s, ew_r, og_s, og_r,
 ):
     dp, row, col = lax.axis_index("dp"), lax.axis_index("row"), lax.axis_index("col")
@@ -68,7 +70,8 @@
     for device in (at_x(1), at_x(-1), sibling, other_dp):
         pl.semaphore_signal(barrier, inc=1, device_id=device, device_id_type=MESH)
     gall[x, p] = g_ref[...]
-    pat[col] = p_ref[...]
+    pat[col, 176:192] = jnp.zeros((16, 128), BF16)
+    pat[col, 0:182] = p_ref[...]
     for h in range(6):
         wt[h] = w_ref[h].T
     pl.semaphore_wait(barrier, 19)
@@ -255,6 +258,18 @@
         inv_buf[n] = inv
         ao[own_head, lax.div(n, 2), lax.rem(n, 2)] = (out * inv).astype(BF16)
 
+    def og_copy(t, k):
+        return remote(og.at[t, k], og_in.at[t, own_head], og_s.at[t, k], og_r.at[t], (dp, row, k))
+
+    def og_send(t, k):
+        @pl.when(k == col)
+        def _():
+            pltpu.make_async_copy(og.at[t, k], og_in.at[t, own_head], og_r.at[t]).start()
+
+        @pl.when(k != col)
+        def _():
+            og_copy(t, k).start()
+
     def bwd_block(n):
         query = queries_of(n)
         c, half = lax.div(n, 2), lax.rem(n, 2)
@@ -272,12 +287,75 @@
             part = plain_dot(k_t[b], ds)
             grad = part if grad is None else grad + part
         og[0, pl.ds(2 * n, 2)] = (grad * FACTOR).T.astype(BF16).reshape(2, 128, DH)
+        for k in range(2):
+            og_send(0, 2 * n + k)
+
+    def ag_copy(kind, h, c, device):
+        return remote(ao.at[h, c], ao.at[h, c], ag_s.at[kind, h, c], ag_r.at[h, c], device)
+
+    def ag_wait(h, c):
+        pltpu.make_async_copy(ao.at[h, c], ao.at[h, c], ag_r.at[h, c]).wait()
+
+    def ow_copy(h):
+        return remote(ow_out.at[h], ow_in.at[h], ow_s.at[h], ow_r.at[h], other_dp)
+
+    def ow_add(h, i, c):
+        part = plain_dot(ao[h, c, 0], gall[c, 0]) + plain_dot(ao[h, c, 1], gall[c, 1])
+
+        @pl.when(i == 0)
+        def _():
+            ow_acc[h] = part
+
+        @pl.when(jnp.logical_and(i > 0, i < 3))
+        def _():
+            ow_acc[h] += part
+
+        @pl.when(i == 3)
+        def _():
+            ow_out[h] = (ow_acc[h] + part).astype(BF16)
+            ow_copy(h).start()
+
+    def ag_item(i, q):
+        c = chunk_of(i)
+        dist = lax.div(q + 1, 2)
+        is_min = (1 - lax.rem(q, 2)) * jnp.minimum(q, 1)
+        t = lax.rem(zp + is_min * dist + (1 - is_min) * (8 - dist), 8)
+        here = q == 0
+        for j in range(2):
+            exists, h = heads_of(t, j)
+
+            @pl.when(exists)
+            def _():
+                root = jnp.logical_and(here, owner_y(h) == y)
+
+                @pl.when(jnp.logical_not(root))
+                def _():
+                    ag_wait(h, c)
+
+                @pl.when(root)
+                def _():
+                    ag_copy(2, h, c, at(1 - y, zp)).start()
+
+                @pl.when(jnp.logical_and(is_min == 0, dist < 4))
+                def _():
+                    ag_copy(0, h, c, at(y, z_up)).start()
+
+                @pl.when(jnp.logical_or(here, jnp.logical_and(is_min == 1, dist < 3)))
+                def _():
+                    ag_copy(1, h, c, at(y, z_down)).start()
+
+                ow_add(h, i, c)
 
     g_wait(x, 1 - p)
 
-    @pl.loop(0, 3 * RS_GAP + 8)
+    @pl.when(is_owner)
+    def _():
+        kacc[...] = jnp.zeros_like(kacc)
+        vacc[...] = jnp.zeros_like(vacc)
+
+    @pl.loop(0, STEPS)
     def _(tau):
-        @pl.when(tau == RS_GAP)
+        @pl.when(tau == 1)
         def _():
             g_wait(x - step_x, p)
             g_start(3)
@@ -287,19 +365,15 @@
             g_wait(x - step_x, 1 - p)
             g_wait(x + step_x, 1 - p)
 
-        @pl.when(tau == 3 * RS_GAP)
+        @pl.when(tau == 3)
         def _():
             g_wait(x + 2, p)
             g_start(6)
             g_wait(x + 2, 1 - p)
 
-        @pl.when(jnp.logical_and(tau >= RS_GAP, tau < RS_GAP + 4))
-        def _():
-            patch_step(tau - RS_GAP + 1)
-
         @pl.loop(0, 4)
         def _(i):
-            q = tau - RS_GAP * i
+            q = tau - i
 
             @pl.when(jnp.logical_and(q >= 0, q < 7))
             def _():
@@ -309,13 +383,46 @@
             def _():
                 rs_root(i)
 
-        @pl.when(jnp.logical_and(is_owner, tau >= FWD_AT))
+        @pl.when(jnp.logical_and(tau >= 2, tau < 6))
+        def _():
+            patch_step(tau - 1)
+
+        @pl.loop(0, 4)
+        def _(i):
+            q = tau - AG_AT - i
+
+            @pl.when(jnp.logical_and(q >= 0, q < 8))
+            def _():
+                ag_item(i, q)
+
+        @pl.when(is_owner)
         def _():
             @pl.when(tau == FWD_AT)
             def _():
                 fwd_setup()
 
-            fwd_block(tau - FWD_AT)
+            @pl.when(jnp.logical_and(tau >= FWD_AT, tau < FWD_AT + 4))
+            def _():
+                @pl.loop(0, 2)
+                def _(half):
+                    fwd_block(2 * chunk_of(tau - FWD_AT) + half)
+
+            @pl.when(jnp.logical_and(tau >= BWD_AT, tau < BWD_AT + 4))
+            def _():
+                @pl.loop(0, 2)
+                def _(half):
+                    bwd_block(2 * chunk_of(tau - BWD_AT) + half)
+
+            @pl.when(tau == SEND_AT)
+            def _():
+                for b in range(4):
+                    og[1, 4 * b : 4 * b + 4] = (kacc[b] * FACTOR).astype(BF16).reshape(4, 128, DH)
+                    og[2, 4 * b : 4 * b + 4] = vacc[b].astype(BF16).reshape(4, 128, DH)
+
+                @pl.loop(0, 16)
+                def _(k):
+                    for t in (1, 2):
+                        og_send(t, lax.rem(col + k, 16))
 
     @pl.loop(0, 8)
     def _(k):
@@ -330,104 +437,18 @@
     ew_copy = remote(ew_out, ew_in, ew_s, ew_r, other_dp)
     ew_copy.start()
 
-    def ag_copy(kind, h, c, device):
-        return remote(ao.at[h, c], ao.at[h, c], ag_s.at[kind, h, c], ag_r.at[h, c], device)
-
-    def ag_wait(h, c):
-        pltpu.make_async_copy(ao.at[h, c], ao.at[h, c], ag_r.at[h, c]).wait()
-
-    def ow_copy(h):
-        return remote(ow_out.at[h], ow_in.at[h], ow_s.at[h], ow_r.at[h], other_dp)
-
-    def finish_head(h):
-        total = None
-        for c in range(4):
-            for half in range(2):
-                part = plain_dot(ao[h, c, half], gall[c, half])
-                total = part if total is None else total + part
-        ow_out[h] = total.astype(BF16)
-        ow_copy(h).start()
-
-    def ag_item(c, q):
-        dist = lax.div(q + 1, 2)
-        is_min = (1 - lax.rem(q, 2)) * jnp.minimum(q, 1)
-        t = lax.rem(zp + is_min * dist + (1 - is_min) * (8 - dist), 8)
-        here = q == 0
-        for j in range(2):
-            exists, h = heads_of(t, j)
-
-            @pl.when(exists)
-            def _():
-                root = jnp.logical_and(here, owner_y(h) == y)
-
-                @pl.when(jnp.logical_not(root))
-                def _():
-                    ag_wait(h, c)
-
-                @pl.when(root)
-                def _():
-                    ag_copy(2, h, c, at(1 - y, zp)).start()
-
-                @pl.when(jnp.logical_and(is_min == 0, dist < 4))
-                def _():
-                    ag_copy(0, h, c, at(y, z_up)).start()
-
-                @pl.when(jnp.logical_or(here, jnp.logical_and(is_min == 1, dist < 3)))
-                def _():
-                    ag_copy(1, h, c, at(y, z_down)).start()
-
-                @pl.when(c == 3)
-                def _():
-                    finish_head(h)
-
-    @pl.when(is_owner)
-    def _():
-        kacc[...] = jnp.zeros_like(kacc)
-        vacc[...] = jnp.zeros_like(vacc)
-
-    @pl.loop(0, 3 * AG_GAP + 8)
-    def _(tau):
-        @pl.loop(0, 4)
-        def _(c):
-            q = tau - AG_GAP * c
-
-            @pl.when(jnp.logical_and(q >= 0, q < 8))
-            def _():
-                ag_item(c, q)
-
-        @pl.when(jnp.logical_and(is_owner, tau < 8))
-        def _():
-            bwd_block(tau)
-
-    def og_copy(t, k):
-        return remote(og.at[t, k], og_in.at[t, own_head], og_s.at[t, k], og_r.at[t], (dp, row, k))
-
-    @pl.when(is_owner)
-    def _():
-        for b in range(4):
-            og[1, 4 * b : 4 * b + 4] = (kacc[b] * FACTOR).astype(BF16).reshape(4, 128, DH)
-            og[2, 4 * b : 4 * b + 4] = vacc[b].astype(BF16).reshape(4, 128, DH)
-
-        for t in range(3):
-            pltpu.make_async_copy(og.at[t, col], og_in.at[t, own_head], og_r.at[t]).start()
-
-        @pl.loop(1, 16)
-        def _(k):
-            for t in range(3):
-                og_copy(t, lax.rem(col + k, 16)).start()
-
     ew_copy.wait()
-    ew_ref[...] = ew_out[...].astype(F32) + ew_in[...].astype(F32)
+    ew_ref[...] = (ew_out[...].astype(F32) + ew_in[...].astype(F32)).astype(BF16)
 
     @pl.loop(0, 6)
     def _(h):
         ow_copy(h).wait()
-        ow_ref[h] = ow_out[h].astype(F32) + ow_in[h].astype(F32)
-
-    for t, ref in enumerate((qg_ref, kg_ref, vg_ref)):
+        ow_ref[h] = (ow_out[h].astype(F32) + ow_in[h].astype(F32)).astype(BF16)
+
+    for t in range(3):
         pltpu.make_async_copy(og_in.at[t], og_in.at[t], og_r.at[t]).wait()
         for h in range(6):
-            ref[:, h * DH : (h + 1) * DH] = og_in[t, h].astype(F32)
+            qkv_ref[t, :, h * DH : (h + 1) * DH] = og_in[t, h]
 
     for h in range(6):
         @pl.when(jnp.logical_not(owns(h)))
@@ -482,8 +503,14 @@
                 og_copy(t, lax.rem(col + k, 16)).wait_send()
 
 
+def widen(qkv_ref, ow_ref, ew_ref, qg_ref, kg_ref, vg_ref, ow_out, ew_out):
+    for t, ref in enumerate((qg_ref, kg_ref, vg_ref)):
+        ref[...] = qkv_ref[t].astype(F32)
+    ow_out[...] = ow_ref[...].astype(F32)
+    ew_out[...] = ew_ref[0:182].astype(F32)
+
+
 def body(patches, queries, attn_keys, attn_values, out_weight, output_grad):
-    patch_t = jnp.pad(patches[0].T, ((0, 10), (0, 0)))
     dma = pltpu.SemaphoreType.DMA
     scratch = [
         pltpu.VMEM((4, 2, 256, 768), BF16),
@@ -501,6 +528,7 @@
         pltpu.VMEM((8, 1, 256), F32),
         pltpu.VMEM((4, 512, DH), F32),
         pltpu.VMEM((4, 512, DH), F32),
+        pltpu.VMEM((6, DH, 768), F32),
         pltpu.VMEM((3, 16, 128, DH), BF16),
         pltpu.VMEM((3, 6, 128, DH), BF16),
         pltpu.VMEM((6, 128, 768), BF16),
@@ -518,22 +546,33 @@
         dma((3, 16)), dma((3,)),
     ]
     vmem = pl.BlockSpec(memory_space=pltpu.VMEM)
-    qg, kg, vg, ow, ew = pl.pallas_call(
+    qkv_grad, ow, ew = pl.pallas_call(
         kernel,
-        out_shape=[jax.ShapeDtypeStruct((128, 768), F32)] * 3
-        + [jax.ShapeDtypeStruct((6, 128, 768), F32), jax.ShapeDtypeStruct((192, 768), F32)],
+        out_shape=[
+            jax.ShapeDtypeStruct((3, 128, 768), BF16),
+            jax.ShapeDtypeStruct((6, DH, 768), BF16),
+            jax.ShapeDtypeStruct((192, 768), BF16),
+        ],
         in_specs=[vmem] * 6,
-        out_specs=[vmem] * 5,
+        out_specs=[vmem] * 3,
         scratch_shapes=scratch,
         compiler_params=pltpu.CompilerParams(
             collective_id=0, has_side_effects=True, vmem_limit_bytes=60 * 2**20
         ),
         cost_estimate=pl.CostEstimate(flops=8 * 10**9, bytes_accessed=8 * 10**6, transcendentals=4 * 10**6),
     )(
-        queries[0], attn_keys[0], attn_values[0], patch_t,
+        queries[0], attn_keys[0], attn_values[0], patches[0].T,
         out_weight.reshape(6, DH, 768), output_grad[0],
     )
-    return (qg[None], kg[None], vg[None], ow.reshape(768, 768), ew[:182])
+    qg, kg, vg, ow, ew = pl.pallas_call(
+        widen,
+        out_shape=[jax.ShapeDtypeStruct((128, 768), F32)] * 3
+        + [jax.ShapeDtypeStruct((768, 768), F32), jax.ShapeDtypeStruct((182, 768), F32)],
+        in_specs=[vmem] * 3,
+        out_specs=[vmem] * 5,
+        compiler_params=pltpu.CompilerParams(vmem_limit_bytes=62 * 2**20),
+    )(qkv_grad, ow.reshape(768, 768), ew)
+    return (qg[None], kg[None], vg[None], ow, ew)
 
 
 def solution(mesh):

time: 192 us -> 156 us (0.81)
  the two profiles are of different devices: /device:TPU:20 before, /device:TPU:6 now
where the time goes in v2:
time: 156 us; the launch traced here: 153 us
  Pallas kernels  153 us (98%)
    pallas_call x1, Pallas kernels, body(): pl.pallas_call(kernel, out_shape=[jax.ShapeDtypeStruct((3, 128, 768), BF1...  149 us
    pallas_call x1, Pallas kernels, body(): pl.pallas_call(widen, out_shape=[jax.ShapeDtypeStruct((128, 768), F32)] *...  3.52 us

profile of v2, /device:TPU:6, one launch (start us, length us, event | category | flops | bytes accessed | tf_op | source)
XLA Modules:
  0.0 153.3 jit_solution(17072811519404780681)
XLA Ops:
  0.6 149.1 %shard_map.101 = (bf16[3,128,768]{2,1,0:T(8,128)(2,1)}, bf16[6,128,768]{2,1,0:T(8,128)(2,1)}, bf16[192,768]{1,0:T(8,128)(2,1)}) custom-call(bf16[128,768]{1,0:T(8,128)(2,1)} %bitcast.18, bf16[128,768]{1,0:T(8,128)(2,1)} %bitcast.19, bf16[128,768]{1,0:T(8,128)(2,1)} %bitcast.20, bf16[182,128]{1,0:T(8,128)(2,1)} %bitcast.21, bf16[6,128,768]{2,1,0:T(8,128)(2,1)} %bitcast.13, ...), custom_call_target="tpu_custom_call" | custom-call | flops 8000000000 | bytes 8000000 | tf_op jit(solution)/shard_map/pallas_call | solution.py:549
  149.8 3.5 %shard_map.102 = (f32[128,768]{1,0:T(8,128)}, f32[128,768]{1,0:T(8,128)}, f32[128,768]{1,0:T(8,128)}, f32[768,768]{1,0:T(8,128)}, f32[182,768]{1,0:T(8,128)}) custom-call(bf16[3,128,768]{2,1,0:T(8,128)(2,1)} %get-tuple-element.13.qkv_ref, bf16[768,768]{1,0:T(8,128)(2,1)} %bitcast.12, bf16[192,768]{1,0:T(8,128)(2,1)} %get-tuple-element.15.ew_ref), custom_call_target="tpu_custom_call" | custom-call | tf_op jit(solution)/shard_map/pallas_call | solution.py:567

commit v3 on v2

--- a/solution.py
+++ b/solution.py
@@ -16,9 +16,11 @@
 OWNER_Z = (0, 0, 2, 4, 4, 6)
 FWD_AT = 1
 AG_AT = 2
-BWD_AT = 7
-SEND_AT = 11
-STEPS = 13
+BWD_AT = 5
+PATCH_AT = 1
+EMBED_AT = 5
+STEPS = 10
+AG_Y = 0
 
 
 def plain_dot(left, right):
@@ -33,12 +35,13 @@
     q_ref, k_ref, v_ref, p_ref, w_ref, g_ref,
     qkv_ref, ow_ref, ew_ref,
     gall, wt, qkv, k_t, v_t, rs_in, rs_y, rs_out, d_out, ao, e_buf, s_buf, inv_buf,
-    kacc, vacc, ow_acc, og, og_in, ow_out, ow_in, pat, ew_out, ew_in,
+    kacc, vacc, ow_acc, og, og_in, ow_out, ow_in, pat, ew_acc, ew_out, ew_in,
     in_s, in_r, g_s, g_r, p_s, p_r, rs_s, rs_r, rsy_r, ag_s, ag_r, ow_s, ow_r, ew_s, ew_r, og_s, og_r,
 ):
     dp, row, col = lax.axis_index("dp"), lax.axis_index("row"), lax.axis_index("col")
     x, p = lax.div(row, 2), lax.rem(row, 2)
-    y, z = lax.div(col, 8), lax.rem(col, 8)
+    real_y, z = lax.div(col, 8), lax.rem(col, 8)
+    y = real_y * (1 - p) + p * (1 - real_y)
 
     def mirror(zz):
         return zz * (1 - p) + p * lax.rem(9 - zz, 8)
@@ -47,7 +50,7 @@
     step_x = 1 - 2 * p
 
     def at(yy, zz):
-        return (dp, row, yy * 8 + mirror(zz))
+        return (dp, row, (yy * (1 - p) + p * (1 - yy)) * 8 + mirror(zz))
 
     def at_x(offset):
         return (dp, lax.rem(x + offset + 4, 4) * 2 + p, col)
@@ -74,6 +77,8 @@
     pat[col, 0:182] = p_ref[...]
     for h in range(6):
         wt[h] = w_ref[h].T
+    ow_acc[...] = jnp.zeros_like(ow_acc)
+    ew_acc[...] = jnp.zeros_like(ew_acc)
     pl.semaphore_wait(barrier, 19)
 
     sources = (q_ref, k_ref, v_ref)
@@ -131,7 +136,7 @@
         pltpu.make_async_copy(pat.at[block], pat.at[block], p_r.at[block]).wait()
 
     def block_at(offset):
-        return y * 8 + mirror(lax.rem(zp + offset + 8, 8))
+        return real_y * 8 + mirror(lax.rem(zp + offset + 8, 8))
 
     p_copy(0, col, at(y, z_up)).start()
     p_copy(1, col, at(y, z_down)).start()
@@ -200,7 +205,7 @@
                     rs_out.at[h, c], rs_in.at[is_min, h, c], rs_s.at[h, c], rs_r.at[is_min, h, c], nxt
                 ).start()
 
-    def rs_root(i):
+    def rs_cross(i):
         c = chunk_of(i)
         for j in range(2):
             exists, h = heads_of(zp, j)
@@ -214,6 +219,9 @@
                 rs_out[h, c] = total.astype(BF16)
                 remote(rs_out.at[h, c], rs_y.at[c], rs_s.at[h, c], rsy_r.at[c], at(1 - y, zp)).start()
 
+    def rs_root(i):
+        c = chunk_of(i)
+
         @pl.when(is_owner)
         def _():
             total = partial(own_head, c)
@@ -221,8 +229,7 @@
             rs_wait(1, own_head, c)
             total = total + rs_in[0, own_head, c].astype(F32) + rs_in[1, own_head, c].astype(F32)
             pltpu.make_async_copy(rs_y.at[c], rs_y.at[c], rsy_r.at[c]).wait()
-            total = total + rs_y[c].astype(F32)
-            d_out[c] = total.astype(BF16)
+            d_out[c] = (total + rs_y[c].astype(F32)).astype(BF16)
 
     def chunk_of(i):
         return lax.rem(x + i + lax.div(i, 2) * (1 - 2 * lax.div(i, 3)), 4)
@@ -302,11 +309,7 @@
     def ow_add(h, i, c):
         part = plain_dot(ao[h, c, 0], gall[c, 0]) + plain_dot(ao[h, c, 1], gall[c, 1])
 
-        @pl.when(i == 0)
-        def _():
-            ow_acc[h] = part
-
-        @pl.when(jnp.logical_and(i > 0, i < 3))
+        @pl.when(i < 3)
         def _():
             ow_acc[h] += part
 
@@ -315,36 +318,72 @@
             ow_out[h] = (ow_acc[h] + part).astype(BF16)
             ow_copy(h).start()
 
+    def ag_place(q):
+        dist = lax.div(q + 1, 2)
+        is_min = (1 - lax.rem(q, 2)) * jnp.minimum(q, 1)
+        return dist, is_min, lax.rem(zp + is_min * dist + (1 - is_min) * (8 - dist), 8)
+
     def ag_item(i, q):
         c = chunk_of(i)
-        dist = lax.div(q + 1, 2)
-        is_min = (1 - lax.rem(q, 2)) * jnp.minimum(q, 1)
-        t = lax.rem(zp + is_min * dist + (1 - is_min) * (8 - dist), 8)
+        dist, is_min, t = ag_place(q)
         here = q == 0
         for j in range(2):
             exists, h = heads_of(t, j)
-
-            @pl.when(exists)
-            def _():
-                root = jnp.logical_and(here, owner_y(h) == y)
+            plane = owner_y(h) == y
+
+            @pl.when(jnp.logical_and(exists, jnp.logical_or(i != AG_Y, plane)))
+            def _():
+                root = jnp.logical_and(here, plane)
 
                 @pl.when(jnp.logical_not(root))
                 def _():
                     ag_wait(h, c)
 
-                @pl.when(root)
-                def _():
-                    ag_copy(2, h, c, at(1 - y, zp)).start()
-
-                @pl.when(jnp.logical_and(is_min == 0, dist < 4))
-                def _():
-                    ag_copy(0, h, c, at(y, z_up)).start()
-
-                @pl.when(jnp.logical_or(here, jnp.logical_and(is_min == 1, dist < 3)))
-                def _():
-                    ag_copy(1, h, c, at(y, z_down)).start()
+                    @pl.when(jnp.logical_and(is_min == 0, dist < 4))
+                    def _():
+                        ag_copy(0, h, c, at(y, z_up)).start()
+
+                    @pl.when(jnp.logical_or(here, jnp.logical_and(is_min == 1, dist < 3)))
+                    def _():
+                        ag_copy(1, h, c, at(y, z_down)).start()
+
+                    @pl.when(i == AG_Y)
+                    def _():
+                        ag_copy(2, h, c, at(1 - y, zp)).start()
 
                 ow_add(h, i, c)
+
+    def ag_across(q):
+        c = chunk_of(AG_Y)
+        t = ag_place(q)[2]
+        for j in range(2):
+            exists, h = heads_of(t, j)
+
+            @pl.when(jnp.logical_and(exists, owner_y(h) != y))
+            def _():
+                ag_wait(h, c)
+                ow_add(h, AG_Y, c)
+
+    ew_copy = remote(ew_out, ew_in, ew_s, ew_r, other_dp)
+
+    def embed_step(c):
+        @pl.when(c == 0)
+        def _():
+            @pl.loop(0, 8)
+            def _(k):
+                p_wait((1 - real_y) * 8 + k)
+
+        part = None
+        for n in range(4):
+            tokens = gall[c, n // 2, (n % 2) * 128 : (n % 2) * 128 + 128]
+            dot = plain_dot(pat[4 * c + n], tokens)
+            part = dot if part is None else part + dot
+        ew_acc[...] += part
+
+        @pl.when(c == 3)
+        def _():
+            ew_out[...] = ew_acc[...].astype(BF16)
+            ew_copy.start()
 
     g_wait(x, 1 - p)
 
@@ -353,47 +392,77 @@
         kacc[...] = jnp.zeros_like(kacc)
         vacc[...] = jnp.zeros_like(vacc)
 
+    def rs_step(tau):
+        @pl.loop(0, 4)
+        def _(i):
+            s = tau - i
+
+            @pl.when(jnp.logical_and(tau == 1, i == 0))
+            def _():
+                g_wait(x - step_x, p)
+                g_start(3)
+                g_start(4)
+
+            @pl.when(jnp.logical_and(tau == 1, i == 1))
+            def _():
+                g_wait(x + step_x, p)
+                g_start(5)
+                g_wait(x - step_x, 1 - p)
+                g_wait(x + step_x, 1 - p)
+
+            @pl.when(jnp.logical_and(tau == 3, i == 3))
+            def _():
+                g_wait(x + 2, p)
+                g_start(6)
+                g_wait(x + 2, 1 - p)
+
+            @pl.loop(0, 2)
+            def _(m):
+                q = 2 * s - 1 + m
+
+                @pl.when(jnp.logical_and(q >= 0, q < 7))
+                def _():
+                    rs_chain(i, q)
+
+            @pl.when(s == 4)
+            def _():
+                rs_cross(i)
+
+            @pl.when(s == 5)
+            def _():
+                rs_root(i)
+
+        @pl.when(jnp.logical_and(tau >= PATCH_AT, tau < PATCH_AT + 4))
+        def _():
+            patch_step(tau - PATCH_AT + 1)
+
+    def ag_step(tau):
+        @pl.loop(0, 2)
+        def _(m):
+            q = 2 * (tau - AG_AT - AG_Y - 2) - 1 + m
+
+            @pl.when(jnp.logical_and(q >= 0, q < 8))
+            def _():
+                ag_across(q)
+
+        @pl.loop(0, 4)
+        def _(i):
+            @pl.loop(0, 2)
+            def _(m):
+                q = 2 * (tau - AG_AT - i) - 1 + m
+
+                @pl.when(jnp.logical_and(q >= 0, q < 8))
+                def _():
+                    ag_item(i, q)
+
     @pl.loop(0, STEPS)
     def _(tau):
-        @pl.when(tau == 1)
-        def _():
-            g_wait(x - step_x, p)
-            g_start(3)
-            g_start(4)
-            g_wait(x + step_x, p)
-            g_start(5)
-            g_wait(x - step_x, 1 - p)
-            g_wait(x + step_x, 1 - p)
-
-        @pl.when(tau == 3)
-        def _():
-            g_wait(x + 2, p)
-            g_start(6)
-            g_wait(x + 2, 1 - p)
-
-        @pl.loop(0, 4)
-        def _(i):
-            q = tau - i
-
-            @pl.when(jnp.logical_and(q >= 0, q < 7))
-            def _():
-                rs_chain(i, q)
-
-            @pl.when(q == 7)
-            def _():
-                rs_root(i)
-
-        @pl.when(jnp.logical_and(tau >= 2, tau < 6))
-        def _():
-            patch_step(tau - 1)
-
-        @pl.loop(0, 4)
-        def _(i):
-            q = tau - AG_AT - i
-
-            @pl.when(jnp.logical_and(q >= 0, q < 8))
-            def _():
-                ag_item(i, q)
+        rs_step(tau)
+        ag_step(tau)
+
+        @pl.when(jnp.logical_and(tau >= EMBED_AT, tau < EMBED_AT + 4))
+        def _():
+            embed_step(tau - EMBED_AT)
 
         @pl.when(is_owner)
         def _():
@@ -407,13 +476,18 @@
                 def _(half):
                     fwd_block(2 * chunk_of(tau - FWD_AT) + half)
 
+                c = chunk_of(tau - FWD_AT)
+                ag_copy(2, own_head, c, at(1 - y, zp)).start()
+                ag_copy(0, own_head, c, at(y, z_up)).start()
+                ag_copy(1, own_head, c, at(y, z_down)).start()
+
             @pl.when(jnp.logical_and(tau >= BWD_AT, tau < BWD_AT + 4))
             def _():
                 @pl.loop(0, 2)
                 def _(half):
                     bwd_block(2 * chunk_of(tau - BWD_AT) + half)
 
-            @pl.when(tau == SEND_AT)
+            @pl.when(tau == BWD_AT + 3)
             def _():
                 for b in range(4):
                     og[1, 4 * b : 4 * b + 4] = (kacc[b] * FACTOR).astype(BF16).reshape(4, 128, DH)
@@ -423,19 +497,6 @@
                 def _(k):
                     for t in (1, 2):
                         og_send(t, lax.rem(col + k, 16))
-
-    @pl.loop(0, 8)
-    def _(k):
-        p_wait((1 - y) * 8 + k)
-
-    def ew_add(k, total):
-        c, n = lax.div(k, 4), lax.rem(k, 4)
-        tokens = gall[c, lax.div(n, 2), pl.ds(pl.multiple_of(lax.rem(n, 2) * 128, 128), 128)]
-        return total + plain_dot(pat[k], tokens)
-
-    ew_out[...] = lax.fori_loop(0, 16, ew_add, jnp.zeros((192, 768), F32)).astype(BF16)
-    ew_copy = remote(ew_out, ew_in, ew_s, ew_r, other_dp)
-    ew_copy.start()
 
     ew_copy.wait()
     ew_ref[...] = (ew_out[...].astype(F32) + ew_in[...].astype(F32)).astype(BF16)
@@ -483,15 +544,19 @@
             def _():
                 pltpu.make_async_copy(rs_out.at[h, c], rs_out.at[h, c], rs_s.at[h, c]).wait()
 
-            @pl.when(root)
+            crossing = c == chunk_of(AG_Y)
+            plane = owner_y(h) == y
+            sends = jnp.logical_or(jnp.logical_not(crossing), plane)
+
+            @pl.when(jnp.logical_or(root, jnp.logical_and(crossing, plane)))
             def _():
                 ag_copy(2, h, c, at(1 - y, zp)).wait_send()
 
-            @pl.when(rel < 4)
+            @pl.when(jnp.logical_and(sends, rel < 4))
             def _():
                 ag_copy(0, h, c, at(y, z_up)).wait_send()
 
-            @pl.when(jnp.logical_or(rel == 0, rel > 5))
+            @pl.when(jnp.logical_and(sends, jnp.logical_or(rel == 0, rel > 5)))
             def _():
                 ag_copy(1, h, c, at(y, z_down)).wait_send()
 
@@ -534,6 +599,7 @@
         pltpu.VMEM((6, 128, 768), BF16),
         pltpu.VMEM((6, 128, 768), BF16),
         pltpu.VMEM((16, 192, 128), BF16),
+        pltpu.VMEM((192, 768), F32),
         pltpu.VMEM((192, 768), BF16),
         pltpu.VMEM((192, 768), BF16),
         dma((3, 6)), dma((3,)),

time: 156 us -> 133 us (0.85); the launches traced: 153 us -> 133 us
  Pallas kernels: 153 us -> 133 us
    pallas_call x1, Pallas kernels: 149 us -> 129 us  [body(): pl.pallas_call(kernel, out_shape=[jax.ShapeDtypeStruct((3, 128, 768), BF1...]
where the time goes in v3:
time: 133 us
  Pallas kernels  133 us (100%)
    pallas_call x1, Pallas kernels, body(): pl.pallas_call(kernel, out_shape=[jax.ShapeDtypeStruct((3, 128, 768), BF1...  129 us
    pallas_call x1, Pallas kernels, body(): pl.pallas_call(widen, out_shape=[jax.ShapeDtypeStruct((128, 768), F32)] *...  3.52 us

profile of v3, /device:TPU:6, one launch (start us, length us, event | category | flops | bytes accessed | tf_op | source)
XLA Modules:
  0.0 133.2 jit_solution(737449359944586249)
XLA Ops:
  0.6 129.1 %shard_map.101 = (bf16[3,128,768]{2,1,0:T(8,128)(2,1)}, bf16[6,128,768]{2,1,0:T(8,128)(2,1)}, bf16[192,768]{1,0:T(8,128)(2,1)}) custom-call(bf16[128,768]{1,0:T(8,128)(2,1)} %bitcast.18, bf16[128,768]{1,0:T(8,128)(2,1)} %bitcast.19, bf16[128,768]{1,0:T(8,128)(2,1)} %bitcast.20, bf16[182,128]{1,0:T(8,128)(2,1)} %bitcast.21, bf16[6,128,768]{2,1,0:T(8,128)(2,1)} %bitcast.13, ...), custom_call_target="tpu_custom_call" | custom-call | flops 8000000000 | bytes 8000000 | tf_op jit(solution)/shard_map/pallas_call | solution.py:615
  129.7 3.5 %shard_map.102 = (f32[128,768]{1,0:T(8,128)}, f32[128,768]{1,0:T(8,128)}, f32[128,768]{1,0:T(8,128)}, f32[768,768]{1,0:T(8,128)}, f32[182,768]{1,0:T(8,128)}) custom-call(bf16[3,128,768]{2,1,0:T(8,128)(2,1)} %get-tuple-element.13.qkv_ref, bf16[768,768]{1,0:T(8,128)(2,1)} %bitcast.12, bf16[192,768]{1,0:T(8,128)(2,1)} %get-tuple-element.15.ew_ref), custom_call_target="tpu_custom_call" | custom-call | tf_op jit(solution)/shard_map/pallas_call | solution.py:633

commit v4 on v3

--- a/solution.py
+++ b/solution.py
@@ -14,12 +14,12 @@
 FACTOR = DH ** (-0.5)
 OWNER_Y = (0, 1, 0, 0, 1, 0)
 OWNER_Z = (0, 0, 2, 4, 4, 6)
-FWD_AT = 1
-AG_AT = 2
+FWD_AT = 0
+AG_AT = 1
 BWD_AT = 5
 PATCH_AT = 1
 EMBED_AT = 5
-STEPS = 10
+STEPS = 9
 AG_Y = 0
 
 
@@ -397,16 +397,16 @@
         def _(i):
             s = tau - i
 
-            @pl.when(jnp.logical_and(tau == 1, i == 0))
+            @pl.when(jnp.logical_and(tau == 0, i == 3))
             def _():
                 g_wait(x - step_x, p)
                 g_start(3)
                 g_start(4)
-
-            @pl.when(jnp.logical_and(tau == 1, i == 1))
-            def _():
                 g_wait(x + step_x, p)
                 g_start(5)
+
+            @pl.when(jnp.logical_and(tau == 1, i == 1))
+            def _():
                 g_wait(x - step_x, 1 - p)
                 g_wait(x + step_x, 1 - p)
 

time: 133 us -> 129 us (0.970)
  Pallas kernels: 133 us -> 128 us
    pallas_call x1, Pallas kernels: 129 us -> 124 us  [body(): pl.pallas_call(kernel, out_shape=[jax.ShapeDtypeStruct((3, 128, 768), BF1...]
where the time goes in v4:
time: 129 us; the launch traced here: 128 us
  Pallas kernels  128 us (99%)
    pallas_call x1, Pallas kernels, body(): pl.pallas_call(kernel, out_shape=[jax.ShapeDtypeStruct((3, 128, 768), BF1...  124 us
    pallas_call x1, Pallas kernels, body(): pl.pallas_call(widen, out_shape=[jax.ShapeDtypeStruct((128, 768), F32)] *...  3.52 us

profile of v4, /device:TPU:6, one launch (start us, length us, event | category | flops | bytes accessed | tf_op | source)
XLA Modules:
  0.0 128.2 jit_solution(657738998351223626)
XLA Ops:
  0.6 124.1 %shard_map.101 = (bf16[3,128,768]{2,1,0:T(8,128)(2,1)}, bf16[6,128,768]{2,1,0:T(8,128)(2,1)}, bf16[192,768]{1,0:T(8,128)(2,1)}) custom-call(bf16[128,768]{1,0:T(8,128)(2,1)} %bitcast.18, bf16[128,768]{1,0:T(8,128)(2,1)} %bitcast.19, bf16[128,768]{1,0:T(8,128)(2,1)} %bitcast.20, bf16[182,128]{1,0:T(8,128)(2,1)} %bitcast.21, bf16[6,128,768]{2,1,0:T(8,128)(2,1)} %bitcast.13, ...), custom_call_target="tpu_custom_call" | custom-call | flops 8000000000 | bytes 8000000 | tf_op jit(solution)/shard_map/pallas_call | solution.py:615
  124.7 3.5 %shard_map.102 = (f32[128,768]{1,0:T(8,128)}, f32[128,768]{1,0:T(8,128)}, f32[128,768]{1,0:T(8,128)}, f32[768,768]{1,0:T(8,128)}, f32[182,768]{1,0:T(8,128)}) custom-call(bf16[3,128,768]{2,1,0:T(8,128)(2,1)} %get-tuple-element.13.qkv_ref, bf16[768,768]{1,0:T(8,128)(2,1)} %bitcast.12, bf16[192,768]{1,0:T(8,128)(2,1)} %get-tuple-element.15.ew_ref), custom_call_target="tpu_custom_call" | custom-call | tf_op jit(solution)/shard_map/pallas_call | solution.py:633
